TPU v7x, 32 devices: a whole 2x2x4 slice. The times are simulated.
32 devices in a mesh: gx: 8 (over z, y), gy: 4 (over x, core).
Axes of the slice: x: 2, y: 2, z: 4, core: 2. Of those that a mesh axis runs over, the one named last changes fastest.
Arguments:
- cotangent: float32 [9, 64, 256, 256], P(None, 'gx', 'gy'), may hold values from -6 to 6
- fields_one: float32 [9, 64, 256, 256], P(None, 'gx', 'gy'), may hold values from 0 to 1
- fields_zero: float32 [9, 64, 256, 256], P(None, 'gx', 'gy'), may hold values from 0 to 1
- slot_grain: int32 [8, 32, 8], P('gx', 'gy'), may hold values from 0 to 255, as said below
Outputs:
- adjoint_fields: float32 [9, 64, 256, 256], P(None, 'gx', 'gy')
- grain_grad: float32 [256, 256], P(('gx', 'gy'))
Inputs may be any that keep to these rules, and one draw needn't show every extreme that they name: `slot_grain`: grain g is owned by device g // 8, devices counted with gx slowest. Every slot of a tile names a grain whose owner has the tile's index along gy. At most 16 of the slots of one device name grains of one owner, and in every draw some owner receives exactly 16 from every device of its gy group.
All inputs are finite; a program needn't handle non-finite values.
Results may differ from a plain program's by a relative error of at most 0.000096.
Values sent between devices are 32-bit elements; how exact they have to be, the bound alone decides.
A program may use at most 128 MiB of HBM per device.

v0:
```python
import jax
import jax.numpy as jnp
from jax import lax
from jax.sharding import PartitionSpec as P

TILE = 8
GRAIN_DEV = 8


time_step = 0.05
well_height = 16.0
barrier = 1.0


def extended_2(block, sides, width):
    for axis, dim in sides:
        count = lax.axis_size(axis)
        forward = [(i, i + 1) for i in range(count - 1)]
        backward = [(target, source) for source, target in forward]
        low = lax.ppermute(
            lax.slice_in_dim(block, block.shape[dim] - width, None, axis=dim), axis, forward
        )
        high = lax.ppermute(lax.slice_in_dim(block, 0, width, axis=dim), axis, backward)
        block = jnp.concatenate([low, block, high], axis=dim)
    return block


def laplace(padded, margin):
    extended = jnp.pad(padded, [(0, 0)] * (padded.ndim - 1) + [(1, 1)])
    span_x = padded.shape[-3] - 2 * margin
    span_y = padded.shape[-2] - 2 * margin
    depth = padded.shape[-1]

    def shifted(step_x, step_y, step_z):
        return extended[
            ...,
            margin + step_x : margin + step_x + span_x,
            margin + step_y : margin + step_y + span_y,
            1 + step_z : 1 + step_z + depth,
        ]

    total = shifted(1, 0, 0) + shifted(-1, 0, 0) + shifted(0, 1, 0) + shifted(0, -1, 0)
    total = total + shifted(0, 0, 1) + shifted(0, 0, -1)
    return total - 6.0 * shifted(0, 0, 0)


def pointwise(costate, fields, lap_costate, lam_mu, lap_mu):
    density = fields[0]
    phases = fields[1:]
    lam_c = costate[0]
    lam_e = costate[1:]
    square_sum = jnp.sum(phases * phases, axis=0)
    weighted = jnp.sum(lam_e * phases, axis=0)
    coupled = jnp.sum(lam_e * (phases * phases - phases), axis=0)
    curvature = well_height * (2.0 - 12.0 * density + 12.0 * density * density) + 2.0 * barrier
    new_density = lam_c + lam_mu * curvature - lap_mu - 12.0 * barrier * time_step * coupled
    inner = (
        lam_e * (1.0 - density - 2.0 * (2.0 - density) * phases + square_sum)
        + 2.0 * phases * weighted
    )
    new_phases = lam_e - 12.0 * barrier * time_step * inner + time_step * lap_costate[1:]
    new_phases = new_phases + 12.0 * barrier * lam_mu * (phases * phases - phases)
    return jnp.concatenate([new_density[None], new_phases], axis=0)


def adjoint_step(costate, fields):
    extended = extended_2(costate, (("gx", 1), ("gy", 2)), 1)
    lap_costate = laplace(extended, 1)
    lam_mu = time_step * lap_costate[0]
    mu_padded = extended_2(lam_mu, (("gx", 0), ("gy", 1)), 1)
    lap_mu = laplace(mu_padded, 1)
    return pointwise(costate, fields, lap_costate, lam_mu, lap_mu)


def tile_rows(phase_costate):
    slots, size_x, size_y, depth = phase_costate.shape
    blocks = phase_costate.reshape(slots, size_x // TILE, TILE, size_y // TILE, TILE, depth)
    summed = jnp.sum(blocks, axis=(2, 4))
    return jnp.transpose(summed, (1, 2, 0, 3)).reshape(-1, depth)


def pack_rows(partial_value, slot_grain):
    grains = slot_grain.reshape(-1)
    row_count = grains.shape[0]
    peer_count = lax.axis_size("gx")
    groups = lax.axis_size("gy")
    capacity = max(2, 2 * row_count // peer_count)
    peer_gx = grains // GRAIN_DEV // groups
    local_id = grains % GRAIN_DEV
    row_index = jnp.arange(row_count)
    before = (peer_gx[None, :] == peer_gx[:, None]) & (row_index[None, :] < row_index[:, None])
    position = jnp.sum(before.astype(jnp.int32), axis=1)
    target = peer_gx * capacity + position
    selector = (jnp.arange(peer_count * capacity)[:, None] == target[None, :]).astype(jnp.float32)
    send_rows = jnp.dot(selector, partial_value, precision=lax.Precision.HIGHEST).reshape(
        peer_count, capacity, -1
    )
    labels = jnp.dot(selector, (local_id + 1).astype(jnp.float32), precision=lax.Precision.HIGHEST)
    return (send_rows, labels.reshape(peer_count, capacity))


def unpack_rows(got_rows, got_labels):
    wanted = (jnp.arange(GRAIN_DEV) + 1).astype(jnp.float32)
    selector = (got_labels.reshape(-1)[None, :] == wanted[:, None]).astype(jnp.float32)
    flat_rows = got_rows.reshape(-1, got_rows.shape[-1])
    return jnp.dot(selector, flat_rows, precision=lax.Precision.HIGHEST)


def shards(cotangent, fields_one, fields_zero, slot_grain):
    costate_one = adjoint_step(cotangent, fields_one)
    adjoint_fields = adjoint_step(costate_one, fields_zero)
    partial_value = time_step * tile_rows(cotangent[1:]) + time_step * tile_rows(costate_one[1:])
    send_rows, labels = pack_rows(partial_value, slot_grain)
    got_rows, got_labels = (
        lax.all_to_all(send_rows, "gx", split_axis=0, concat_axis=0, tiled=True),
        lax.all_to_all(labels, "gx", split_axis=0, concat_axis=0, tiled=True),
    )
    grain_grad = unpack_rows(got_rows, got_labels)
    return (adjoint_fields, grain_grad)


def solution(mesh):
    placed = (
        P(None, "gx", "gy", None),
        P(None, "gx", "gy", None),
        P(None, "gx", "gy", None),
        P("gx", "gy", None),
    )
    return jax.shard_map(
        shards,
        mesh=mesh,
        in_specs=placed,
        out_specs=(P(None, "gx", "gy", None), P(("gx", "gy"), None)),
        check_vma=False,
    )
```

profile of v0, /device:TPU:10, one launch (start us, length us, event | category | flops | bytes accessed | tf_op | source)
XLA Modules:
  0.0 169.7 jit_solution(14788934756765013218)
XLA Ops:
  0.6 2.4 %fusion.61 = (f32[9,1,64,256]{3,2,1,0:T(8,128)}, f32[9,1,64,256]{3,2,1,0:T(8,128)}) fusion(f32[9,8,64,256]{3,2,1,0:T(8,128)} %param.4), kind=kLoop, calls=%fused_computation.187 | loop fusion | bytes 2359296 | tf_op jit(solution)/shard_map/slice | solution.py:23
  3.0 3.4 %collective-permute-start.1 = (f32[9,1,64,256]{3,2,1,0:T(8,128)}, f32[9,1,64,256]{3,2,1,0:T(8,128)S(1)}, u32[]{:S(2)}, u32[]{:S(2)}) collective-permute-start(f32[9,1,64,256]{3,2,1,0:T(8,128)} %get-tuple-element.30), channel_id=1, source_target_pairs={{0,4},{4,8},{8,12},{12,16},{16,20},{20,24},{24,28},{1,5},{5,9},{9,... | collective-permute-start | bytes 1769480 | tf_op jit(solution)/shard_map/ppermute | solution.py:20
  6.4 3.3 %collective-permute-start = (f32[9,1,64,256]{3,2,1,0:T(8,128)}, f32[9,1,64,256]{3,2,1,0:T(8,128)S(1)}, u32[]{:S(2)}, u32[]{:S(2)}) collective-permute-start(f32[9,1,64,256]{3,2,1,0:T(8,128)} %get-tuple-element.29), channel_id=1, source_target_pairs={{4,0},{8,4},{12,8},{16,12},{20,16},{24,20},{28,24},{5,1},{9,5},{13... | collective-permute-start | bytes 1769480 | tf_op jit(solution)/shard_map/ppermute | solution.py:23
  9.7 0.8 reshape.180
  10.5 0.7 fusion.52
  11.2 0.2 convert_reduce_fusion
  11.4 0.1 reshape.182
  11.5 1.0 convolution_bitcast_fusion
  12.5 5.5 %all-to-all-start = ((f32[8,1,16]{2,1,0:T(1,128)}), f32[8,1,16]{2,1,0:T(1,128)S(1)}, u32[]{:S(2)}, u32[]{:S(2)}) async-start(f32[8,1,16]{2,1,0:T(1,128)} %convolution_bitcast_fusion), calls=%async_computation | async-start | bytes 8192 | tf_op jit(solution)/shard_map/all_to_all | solution.py:116
  18.1 5.2 %multiply_reduce_fusion.4 = (f32[8,64,256]{2,1,0:T(8,128)S(1)}, f32[8,64,256]{2,1,0:T(8,128)S(1)}, f32[8,64,256]{2,1,0:T(8,128)S(1)}, f32[8,64,256]{2,1,0:T(8,128)}) fusion(f32[9,8,64,256]{3,2,1,0:T(8,128)} %param.5, f32[9,8,64,256]{3,2,1,0:T(8,128)} %param.4), kind=kLoop, calls=%fused_computation.57 | loop fusion | flops 7864320 | bytes 10485760 | tf_op jit(solution)/shard_map/reduce_sum | solution.py:53
  23.3 2.1 %subtract_bitcast_fusion.1 = (f32[8,64,256]{2,1,0:T(8,128)}, f32[8,64,256]{2,1,0:T(8,128)}) fusion(f32[9,8,64,256]{3,2,1,0:T(8,128)} %param.5), kind=kLoop, calls=%fused_computation.128 | loop fusion | flops 393216 | bytes 1572864 | tf_op jit(solution)/shard_map/sub | solution.py:58
  25.4 1.9 %subtract_bitcast_fusion = (f32[8,64,256]{2,1,0:T(8,128)S(1)}, f32[8,64,256]{2,1,0:T(8,128)}) fusion(f32[9,8,64,256]{3,2,1,0:T(8,128)} %param.6), kind=kLoop, calls=%fused_computation.125 | loop fusion | flops 393216 | bytes 1572864 | tf_op jit(solution)/shard_map/sub | solution.py:58
  27.3 0.8 broadcast_multiply_fusion
  28.1 3.8 %collective-permute-done.1 = f32[9,1,64,256]{3,2,1,0:T(8,128)S(1)} collective-permute-done((f32[9,1,64,256]{3,2,1,0:T(8,128)}, f32[9,1,64,256]{3,2,1,0:T(8,128)S(1)}, u32[]{:S(2)}, u32[]{:S(2)}) %collective-permute-start.1) | collective-permute-done | bytes 589856 | tf_op jit(solution)/shard_map/ppermute | solution.py:20
  32.1 0.7 constant_dynamic-update-slice_fusion.1
  32.7 1.0 collective-permute-done
  33.8 0.1 fusion.60
  33.9 2.1 %collective-permute-start.2 = (f32[9,10,1,256]{3,1,2,0:T(8,128)S(1)}, f32[9,10,1,256]{3,1,2,0:T(8,128)S(1)}, u32[]{:S(2)}, u32[]{:S(2)}) collective-permute-start(f32[9,10,1,256]{3,1,2,0:T(8,128)S(1)} %copy.68), channel_id=1, source_target_pairs={{1,0},{2,1},{3,2},{5,4},{6,5},{7,6},{9,8},{10,9},{11,10},{13,12},{... | collective-permute-start | bytes 276488 | tf_op jit(solution)/shard_map/ppermute | solution.py:23
  36.0 2.3 %collective-permute-start.3 = (f32[9,10,1,256]{3,1,2,0:T(8,128)S(1)}, f32[9,10,1,256]{3,1,2,0:T(8,128)S(1)}, u32[]{:S(2)}, u32[]{:S(2)}) collective-permute-start(f32[9,10,1,256]{3,1,2,0:T(8,128)S(1)} %copy.70), channel_id=1, source_target_pairs={{0,1},{1,2},{2,3},{4,5},{5,6},{6,7},{8,9},{9,10},{10,11},{12,13},{... | collective-permute-start | bytes 276488 | tf_op jit(solution)/shard_map/ppermute | solution.py:20
  38.3 0.1 bitcast_reduce_fusion.1
  38.5 0.2 collective-permute-done.2
  38.7 0.1 copy.69
  38.8 3.7 %collective-permute-done.3 = f32[9,10,1,256]{3,1,2,0:T(8,128)S(1)} collective-permute-done((f32[9,10,1,256]{3,1,2,0:T(8,128)S(1)}, f32[9,10,1,256]{3,1,2,0:T(8,128)S(1)}, u32[]{:S(2)}, u32[]{:S(2)}) %collective-permute-start.3) | collective-permute-done | bytes 92192 | tf_op jit(solution)/shard_map/ppermute | solution.py:20
  42.5 0.1 copy.71
  42.6 4.9 %select_maximum_fusion.5 = f32[9,10,66,258]{3,2,1,0:T(8,128)S(1)} fusion(f32[9,10,1,256]{3,2,1,0:T(1,128)S(1)} %copy.69, f32[9,10,64,256]{3,2,1,0:T(8,128)S(1)} %constant_dynamic-update-slice_fusion, f32[9,10,1,256]{3,2,1,0:T(1,128)S(1)} %copy.71), kind=kLoop, calls=%fused_computation.7 | loop fusion | flops 12260160 | bytes 12212640 | tf_op jit(solution)/shard_map/concatenate | solution.py:24
  47.5 6.2 %fusion.6 = f32[9,8,64,256]{3,2,1,0:T(8,128)} fusion(f32[9,10,66,258]{3,2,1,0:T(8,128)S(1)} %select_maximum_fusion.5, f32[9,10,64,256]{3,2,1,0:T(8,128)S(1)} %constant_dynamic-update-slice_fusion, f32[9,10,1,256]{3,2,1,0:T(1,128)S(1)} %copy.71, f32[9,10,1,256]{3,2,1,0:T(1,128)S(1)} %copy.69, f32[9,8,64,256]{3,2,1,0:T(8,128)S(1)} %bitcast.60, ...), kind=kLoop, calls=%fused_computation.37 | loop fusion | flops 12976128 | bytes 26136576 | tf_op jit(solution)/shard_map/sub | solution.py:44
  53.7 1.2 multiply_bitcast_fusion.2
  54.9 3.0 %collective-permute-start.4 = (f32[1,64,256]{2,1,0:T(8,128)S(1)}, f32[1,64,256]{2,1,0:T(8,128)S(1)}, u32[]{:S(2)}, u32[]{:S(2)}) collective-permute-start(f32[1,64,256]{2,1,0:T(8,128)S(1)} %get-tuple-element.38), channel_id=1, source_target_pairs={{4,0},{8,4},{12,8},{16,12},{20,16},{24,20},{28,24},{5,1},{9,5},{13... | collective-permute-start | bytes 196616 | tf_op jit(solution)/shard_map/ppermute | solution.py:23
  58.0 2.8 %collective-permute-start.5 = (f32[1,64,256]{2,1,0:T(8,128)S(1)}, f32[1,64,256]{2,1,0:T(8,128)S(1)}, u32[]{:S(2)}, u32[]{:S(2)}) collective-permute-start(f32[1,64,256]{2,1,0:T(8,128)S(1)} %get-tuple-element.37), channel_id=1, source_target_pairs={{0,4},{4,8},{8,12},{12,16},{16,20},{20,24},{24,28},{1,5},{5,9},{9,... | collective-permute-start | bytes 196616 | tf_op jit(solution)/shard_map/ppermute | solution.py:20
  60.8 0.5 broadcast.394
  61.3 0.7 reduce.9
  62.0 0.1 eq.65
  62.1 3.0 %collective-permute-done.5 = f32[1,64,256]{2,1,0:T(8,128)S(1)} collective-permute-done((f32[1,64,256]{2,1,0:T(8,128)S(1)}, f32[1,64,256]{2,1,0:T(8,128)S(1)}, u32[]{:S(2)}, u32[]{:S(2)}) %collective-permute-start.5) | collective-permute-done | bytes 65568 | tf_op jit(solution)/shard_map/ppermute | solution.py:20
  65.0 1.9 %collective-permute-start.6 = (f32[10,1,256]{2,1,0:T(1,128)S(1)}, f32[10,1,256]{2,1,0:T(1,128)S(1)}, u32[]{:S(2)}, u32[]{:S(2)}) collective-permute-start(f32[10,1,256]{2,1,0:T(1,128)S(1)} %get-tuple-element.34), channel_id=1, source_target_pairs={{1,0},{2,1},{3,2},{5,4},{6,5},{7,6},{9,8},{10,9},{11,10},{13,12},{... | collective-permute-start | bytes 30728 | tf_op jit(solution)/shard_map/ppermute | solution.py:23
  67.0 2.4 %collective-permute-start.7 = (f32[10,1,256]{2,1,0:T(1,128)S(1)}, f32[10,1,256]{2,1,0:T(1,128)S(1)}, u32[]{:S(2)}, u32[]{:S(2)}) collective-permute-start(f32[10,1,256]{2,1,0:T(1,128)S(1)} %get-tuple-element.33), channel_id=1, source_target_pairs={{0,1},{1,2},{2,3},{4,5},{5,6},{6,7},{8,9},{9,10},{10,11},{12,13},{... | collective-permute-start | bytes 30728 | tf_op jit(solution)/shard_map/ppermute | solution.py:20
  69.4 9.3 %multiply_reduce_fusion.3 = (f32[8,64,256]{2,1,0:T(8,128)}, f32[8,64,256]{2,1,0:T(8,128)S(1)}, f32[8,64,256]{2,1,0:T(8,128)}, f32[8,64,256]{2,1,0:T(8,128)S(1)}, f32[8,8,64,256]{3,2,1,0:T(8,128)S(1)}) fusion(f32[9,8,64,256]{3,2,1,0:T(8,128)} %param.6, f32[8,64,256]{2,1,0:T(8,128)S(1)} %get-tuple-element.26, f32[9,8,64,256]{3,2,1,0:T(8,128)} %fusion.6, ...), kind=kLoop, calls=%fused_computation.56 | loop fusion | flops 22544384 | bytes 25690112 | tf_op jit(solution)/shard_map/reduce_sum | solution.py:54
  78.7 0.5 select_maximum_fusion.11
  79.1 2.9 %fusion.23 = f32[8,64,256]{2,1,0:T(8,128)S(1)} fusion(f32[8,64,256]{2,1,0:T(8,128)S(1)} %get-tuple-element.27, f32[10,66,258]{2,1,0:T(8,128)S(1)} %select_maximum_fusion.11, f32[10,1,256]{2,1,0:T(1,128)S(1)} %collective-permute-done.7, f32[1,64,256]{2,1,0:T(8,128)S(1)} %collective-permute-done.4, f32[1,64,256]{2,1,0:T(8,128)S(1)} %collective-permute-done.5, ...), kind=kLoop, calls=%fused_computation.84 | loop fusion | flops 3407872 | bytes 4345856 | tf_op jit(solution)/shard_map/sub | solution.py:56
  82.0 0.1 fusion.16
  82.1 1.9 %collective-permute-start.8 = (f32[9,1,64,256]{3,2,1,0:T(8,128)S(1)}, f32[9,1,64,256]{3,2,1,0:T(8,128)S(1)}, u32[]{:S(2)}, u32[]{:S(2)}) collective-permute-start(f32[9,1,64,256]{3,2,1,0:T(8,128)S(1)} %get-tuple-element.23), channel_id=1, source_target_pairs={{4,0},{8,4},{12,8},{16,12},{20,16},{24,20},{28,24},{5,1},{9,5},{13... | collective-permute-start | bytes 1769480 | tf_op jit(solution)/shard_map/ppermute | solution.py:23
  84.1 3.9 %collective-permute-start.9 = (f32[9,1,64,256]{3,2,1,0:T(8,128)S(1)}, f32[9,1,64,256]{3,2,1,0:T(8,128)S(1)}, u32[]{:S(2)}, u32[]{:S(2)}) collective-permute-start(f32[9,1,64,256]{3,2,1,0:T(8,128)S(1)} %get-tuple-element.22), channel_id=1, source_target_pairs={{0,4},{4,8},{8,12},{12,16},{16,20},{20,24},{24,28},{1,5},{5,9},{9,... | collective-permute-start | bytes 1769480 | tf_op jit(solution)/shard_map/ppermute | solution.py:20
  88.0 0.1 bitcast_reduce_fusion
  88.2 0.8 broadcast_multiply_fusion.1
  89.0 22.3 %collective-permute-done.8 = f32[9,1,64,256]{3,2,1,0:T(8,128)S(1)} collective-permute-done((f32[9,1,64,256]{3,2,1,0:T(8,128)S(1)}, f32[9,1,64,256]{3,2,1,0:T(8,128)S(1)}, u32[]{:S(2)}, u32[]{:S(2)}) %collective-permute-start.8) | collective-permute-done | bytes 589856 | tf_op jit(solution)/shard_map/ppermute | solution.py:23
  111.3 0.1 pad_maximum_fusion.34
  111.5 1.9 %collective-permute-start.10 = (f32[9,10,1,256]{3,1,2,0:T(8,128)S(1)}, f32[9,10,1,256]{3,1,2,0:T(8,128)S(1)}, u32[]{:S(2)}, u32[]{:S(2)}) collective-permute-start(f32[9,10,1,256]{3,1,2,0:T(8,128)S(1)} %copy.74), channel_id=1, source_target_pairs={{1,0},{2,1},{3,2},{5,4},{6,5},{7,6},{9,8},{10,9},{11,10},{13,12},{... | collective-permute-start | bytes 276488 | tf_op jit(solution)/shard_map/ppermute | solution.py:23
  113.4 2.4 %collective-permute-start.11 = (f32[9,10,1,256]{3,1,2,0:T(8,128)S(1)}, f32[9,10,1,256]{3,1,2,0:T(8,128)S(1)}, u32[]{:S(2)}, u32[]{:S(2)}) collective-permute-start(f32[9,10,1,256]{3,1,2,0:T(8,128)S(1)} %copy.76), channel_id=1, source_target_pairs={{0,1},{1,2},{2,3},{4,5},{5,6},{6,7},{8,9},{9,10},{10,11},{12,13},{... | collective-permute-start | bytes 276488 | tf_op jit(solution)/shard_map/ppermute | solution.py:20
  115.8 0.9 fusion.40
  116.7 5.3 %all-to-all-start.1 = ((f32[8,16,256]{2,1,0:T(8,128)}), f32[8,16,256]{2,1,0:T(8,128)}, u32[]{:S(2)}, u32[]{:S(2)}) async-start(f32[8,16,256]{2,1,0:T(8,128)} %fusion.40), calls=%async_computation.1 | async-start | bytes 262144 | tf_op jit(solution)/shard_map/all_to_all | solution.py:115
  122.1 0.1 copy.75
  122.2 0.1 copy.77
  122.3 10.3 %select_maximum_fusion = f32[9,10,66,258]{3,2,1,0:T(8,128)} fusion(f32[9,10,1,256]{3,2,1,0:T(1,128)S(1)} %copy.75, f32[9,10,1,256]{3,2,1,0:T(1,128)S(1)} %copy.77, f32[9,1,64,256]{3,2,1,0:T(8,128)S(1)} %collective-permute-done.8, f32[9,1,64,256]{3,2,1,0:T(8,128)S(1)} %collective-permute-done.9, f32[8,8,64,256]{3,2,1,0:T(8,128)} %copy-done, ...), kind=kLoop, calls=%fused_computation.2 | loop fusion | flops 21455280 | bytes 12212640 | tf_op jit(solution)/shard_map/concatenate | solution.py:24
  132.6 10.3 %fusion.2 = f32[9,8,64,256]{3,2,1,0:T(8,128)} fusion(f32[1,8,64,256]{3,2,1,0:T(8,128)S(1)} %bitcast.64, f32[9,10,66,258]{3,2,1,0:T(8,128)} %select_maximum_fusion, f32[9,10,1,256]{3,2,1,0:T(1,128)S(1)} %copy.77, f32[9,1,64,256]{3,2,1,0:T(8,128)S(1)} %collective-permute-done.8, f32[9,1,64,256]{3,2,1,0:T(8,128)S(1)} %collective-permute-done.9, ...), kind=kLoop, calls=%fused_computation.18 | loop fusion | flops 23592960 | bytes 20238336 | tf_op jit(solution)/shard_map/sub | solution.py:44
  142.9 1.2 slice_multiply_fusion.2
  144.1 3.4 %collective-permute-start.12 = (f32[1,64,256]{2,1,0:T(8,128)S(1)}, f32[1,64,256]{2,1,0:T(8,128)S(1)}, u32[]{:S(2)}, u32[]{:S(2)}) collective-permute-start(f32[1,64,256]{2,1,0:T(8,128)S(1)} %get-tuple-element.36), channel_id=1, source_target_pairs={{4,0},{8,4},{12,8},{16,12},{20,16},{24,20},{28,24},{5,1},{9,5},{13... | collective-permute-start | bytes 196616 | tf_op jit(solution)/shard_map/ppermute | solution.py:23
  147.5 2.5 %collective-permute-start.13 = (f32[1,64,256]{2,1,0:T(8,128)S(1)}, f32[1,64,256]{2,1,0:T(8,128)S(1)}, u32[]{:S(2)}, u32[]{:S(2)}) collective-permute-start(f32[1,64,256]{2,1,0:T(8,128)S(1)} %get-tuple-element.35), channel_id=1, source_target_pairs={{0,4},{4,8},{8,12},{12,16},{16,20},{20,24},{24,28},{1,5},{5,9},{9,... | collective-permute-start | bytes 196616 | tf_op jit(solution)/shard_map/ppermute | solution.py:20
  150.0 1.7 %fusion.53 = f32[8,256]{1,0:T(8,128)} fusion(f32[128,256]{1,0:T(8,128)} %bitcast.29, f32[128]{0:T(128)S(1)} %eq.65, f32[8]{0:T(128)S(1)} %add_convert_fusion), kind=kOutput, calls=%fused_computation.170 | convolution fusion | flops 3146752 | bytes 139808 | tf_op jit(solution)/shard_map/dot_general | solution.py:106
  151.7 2.9 %collective-permute-done.13 = f32[1,64,256]{2,1,0:T(8,128)S(1)} collective-permute-done((f32[1,64,256]{2,1,0:T(8,128)S(1)}, f32[1,64,256]{2,1,0:T(8,128)S(1)}, u32[]{:S(2)}, u32[]{:S(2)}) %collective-permute-start.13) | collective-permute-done | bytes 65568 | tf_op jit(solution)/shard_map/ppermute | solution.py:20
  154.6 1.9 %collective-permute-start.14 = (f32[10,1,256]{2,1,0:T(1,128)S(1)}, f32[10,1,256]{2,1,0:T(1,128)S(1)}, u32[]{:S(2)}, u32[]{:S(2)}) collective-permute-start(f32[10,1,256]{2,1,0:T(1,128)S(1)} %get-tuple-element.32), channel_id=1, source_target_pairs={{1,0},{2,1},{3,2},{5,4},{6,5},{7,6},{9,8},{10,9},{11,10},{13,12},{... | collective-permute-start | bytes 30728 | tf_op jit(solution)/shard_map/ppermute | solution.py:23
  156.5 2.4 %collective-permute-start.15 = (f32[10,1,256]{2,1,0:T(1,128)S(1)}, f32[10,1,256]{2,1,0:T(1,128)S(1)}, u32[]{:S(2)}, u32[]{:S(2)}) collective-permute-start(f32[10,1,256]{2,1,0:T(1,128)S(1)} %get-tuple-element.31), channel_id=1, source_target_pairs={{0,1},{1,2},{2,3},{4,5},{5,6},{6,7},{8,9},{9,10},{10,11},{12,13},{... | collective-permute-start | bytes 30728 | tf_op jit(solution)/shard_map/ppermute | solution.py:20
  158.9 6.0 %fusion.11 = f32[8,8,64,256]{3,2,1,0:T(8,128)S(1)} fusion(f32[9,8,64,256]{3,2,1,0:T(8,128)} %fusion.2, f32[8,8,64,256]{3,2,1,0:T(8,128)} %copy-done, f32[9,8,64,256]{3,2,1,0:T(8,128)} %param.6, f32[8,64,256]{2,1,0:T(8,128)S(1)} %get-tuple-element.19, f32[8,64,256]{2,1,0:T(8,128)} %broadcast_multiply_fusion.1, f32[8,64,256]{2,1,0:T(8,128)} %get-tuple-element.10, ...), kind=kLoop, calls=%fused_computation.51 | loop fusion | flops 14680064 | bytes 19398656 | tf_op jit(solution)/shard_map/add | solution.py:62
  165.0 0.5 select_maximum_fusion.7
  165.5 1.8 %fusion.31 = f32[1,8,64,256]{3,2,1,0:T(8,128)S(1)} fusion(f32[8,64,256]{2,1,0:T(8,128)S(1)} %fusion.23, f32[8,64,256]{2,1,0:T(8,128)S(1)} %get-tuple-element.18, f32[10,66,258]{2,1,0:T(8,128)S(1)} %select_maximum_fusion.7, f32[10,1,256]{2,1,0:T(1,128)S(1)} %collective-permute-done.15, f32[1,64,256]{2,1,0:T(8,128)S(1)} %collective-permute-done.12, ...), kind=kLoop, calls=%fused_computation.92 | loop fusion | flops 3407872 | bytes 4345856 | tf_op jit(solution)/shard_map/broadcast_in_dim | solution.py:63
  167.3 2.5 %pad_maximum_fusion.17 = f32[9,8,64,256]{3,2,1,0:T(8,128)} fusion(f32[8,8,64,256]{3,2,1,0:T(8,128)S(1)} %fusion.11, f32[1,8,64,256]{3,2,1,0:T(8,128)S(1)} %fusion.31), kind=kLoop, calls=%fused_computation.46 | loop fusion | flops 1179648 | bytes 9437184 | tf_op jit(solution)/shard_map/concatenate | solution.py:63
  (37 shorter events, 0.3 us)
Async XLA Ops:
  3.0 29.0 %collective-permute-start.1 = (f32[9,1,64,256]{3,2,1,0:T(8,128)}, f32[9,1,64,256]{3,2,1,0:T(8,128)S(1)}, u32[]{:S(2)}, u32[]{:S(2)}) collective-permute-start(f32[9,1,64,256]{3,2,1,0:T(8,128)} %get-tuple-element.30), channel_id=1, source_target_pairs={{0,4},{4,8},{8,12},{12,16},{16,20},{20,24},{24,28},{1,5},{5,9},{9,... | collective-permute-start | bytes 1769480 | tf_op jit(solution)/shard_map/ppermute | solution.py:20
  6.4 27.3 %collective-permute-start = (f32[9,1,64,256]{3,2,1,0:T(8,128)}, f32[9,1,64,256]{3,2,1,0:T(8,128)S(1)}, u32[]{:S(2)}, u32[]{:S(2)}) collective-permute-start(f32[9,1,64,256]{3,2,1,0:T(8,128)} %get-tuple-element.29), channel_id=1, source_target_pairs={{4,0},{8,4},{12,8},{16,12},{20,16},{24,20},{28,24},{5,1},{9,5},{13... | collective-permute-start | bytes 1769480 | tf_op jit(solution)/shard_map/ppermute | solution.py:23
  12.5 19.5 %slice-start = ((s8[4718592]{0:T(1024)(128)(4,1)}), s8[524288]{0:T(1024)(128)(4,1)S(1)}, s32[]{:S(2)}) async-start(s8[4718592]{0:T(1024)(128)(4,1)} %bitcast.59), calls=%async_computation.2 | async-start | bytes 1048576
  12.5 48.3 %all-to-all-start = ((f32[8,1,16]{2,1,0:T(1,128)}), f32[8,1,16]{2,1,0:T(1,128)S(1)}, u32[]{:S(2)}, u32[]{:S(2)}) async-start(f32[8,1,16]{2,1,0:T(1,128)} %convolution_bitcast_fusion), calls=%async_computation | async-start | bytes 8192 | tf_op jit(solution)/shard_map/all_to_all | solution.py:116
  18.1 14.0 %slice-start.1 = ((s8[4718592]{0:T(1024)(128)(4,1)}), s8[4194304]{0:T(1024)(128)(4,1)S(1)}, s32[]{:S(2)}) async-start(s8[4718592]{0:T(1024)(128)(4,1)} %bitcast.59), calls=%async_computation.3 | async-start | bytes 8388608
  33.9 4.7 %collective-permute-start.2 = (f32[9,10,1,256]{3,1,2,0:T(8,128)S(1)}, f32[9,10,1,256]{3,1,2,0:T(8,128)S(1)}, u32[]{:S(2)}, u32[]{:S(2)}) collective-permute-start(f32[9,10,1,256]{3,1,2,0:T(8,128)S(1)} %copy.68), channel_id=1, source_target_pairs={{1,0},{2,1},{3,2},{5,4},{6,5},{7,6},{9,8},{10,9},{11,10},{13,12},{... | collective-permute-start | bytes 276488 | tf_op jit(solution)/shard_map/ppermute | solution.py:23
  36.0 6.5 %collective-permute-start.3 = (f32[9,10,1,256]{3,1,2,0:T(8,128)S(1)}, f32[9,10,1,256]{3,1,2,0:T(8,128)S(1)}, u32[]{:S(2)}, u32[]{:S(2)}) collective-permute-start(f32[9,10,1,256]{3,1,2,0:T(8,128)S(1)} %copy.70), channel_id=1, source_target_pairs={{0,1},{1,2},{2,3},{4,5},{5,6},{6,7},{8,9},{9,10},{10,11},{12,13},{... | collective-permute-start | bytes 276488 | tf_op jit(solution)/shard_map/ppermute | solution.py:20
  54.9 7.1 %collective-permute-start.4 = (f32[1,64,256]{2,1,0:T(8,128)S(1)}, f32[1,64,256]{2,1,0:T(8,128)S(1)}, u32[]{:S(2)}, u32[]{:S(2)}) collective-permute-start(f32[1,64,256]{2,1,0:T(8,128)S(1)} %get-tuple-element.38), channel_id=1, source_target_pairs={{4,0},{8,4},{12,8},{16,12},{20,16},{24,20},{28,24},{5,1},{9,5},{13... | collective-permute-start | bytes 196616 | tf_op jit(solution)/shard_map/ppermute | solution.py:23
  58.0 7.1 %collective-permute-start.5 = (f32[1,64,256]{2,1,0:T(8,128)S(1)}, f32[1,64,256]{2,1,0:T(8,128)S(1)}, u32[]{:S(2)}, u32[]{:S(2)}) collective-permute-start(f32[1,64,256]{2,1,0:T(8,128)S(1)} %get-tuple-element.37), channel_id=1, source_target_pairs={{0,4},{4,8},{8,12},{12,16},{16,20},{20,24},{24,28},{1,5},{5,9},{9,... | collective-permute-start | bytes 196616 | tf_op jit(solution)/shard_map/ppermute | solution.py:20
  65.0 13.6 %collective-permute-start.6 = (f32[10,1,256]{2,1,0:T(1,128)S(1)}, f32[10,1,256]{2,1,0:T(1,128)S(1)}, u32[]{:S(2)}, u32[]{:S(2)}) collective-permute-start(f32[10,1,256]{2,1,0:T(1,128)S(1)} %get-tuple-element.34), channel_id=1, source_target_pairs={{1,0},{2,1},{3,2},{5,4},{6,5},{7,6},{9,8},{10,9},{11,10},{13,12},{... | collective-permute-start | bytes 30728 | tf_op jit(solution)/shard_map/ppermute | solution.py:23
  67.0 11.7 %collective-permute-start.7 = (f32[10,1,256]{2,1,0:T(1,128)S(1)}, f32[10,1,256]{2,1,0:T(1,128)S(1)}, u32[]{:S(2)}, u32[]{:S(2)}) collective-permute-start(f32[10,1,256]{2,1,0:T(1,128)S(1)} %get-tuple-element.33), channel_id=1, source_target_pairs={{0,1},{1,2},{2,3},{4,5},{5,6},{6,7},{8,9},{9,10},{10,11},{12,13},{... | collective-permute-start | bytes 30728 | tf_op jit(solution)/shard_map/ppermute | solution.py:20
  78.6 32.7 %copy-start = (f32[8,8,64,256]{3,2,1,0:T(8,128)}, f32[8,8,64,256]{3,2,1,0:T(8,128)S(1)}, u32[]{:S(2)}) copy-start(f32[8,8,64,256]{3,2,1,0:T(8,128)S(1)} %get-tuple-element.12) | copy-start | bytes 12582916
  82.1 29.2 %collective-permute-start.8 = (f32[9,1,64,256]{3,2,1,0:T(8,128)S(1)}, f32[9,1,64,256]{3,2,1,0:T(8,128)S(1)}, u32[]{:S(2)}, u32[]{:S(2)}) collective-permute-start(f32[9,1,64,256]{3,2,1,0:T(8,128)S(1)} %get-tuple-element.23), channel_id=1, source_target_pairs={{4,0},{8,4},{12,8},{16,12},{20,16},{24,20},{28,24},{5,1},{9,5},{13... | collective-permute-start | bytes 1769480 | tf_op jit(solution)/shard_map/ppermute | solution.py:23
  84.1 27.2 %collective-permute-start.9 = (f32[9,1,64,256]{3,2,1,0:T(8,128)S(1)}, f32[9,1,64,256]{3,2,1,0:T(8,128)S(1)}, u32[]{:S(2)}, u32[]{:S(2)}) collective-permute-start(f32[9,1,64,256]{3,2,1,0:T(8,128)S(1)} %get-tuple-element.22), channel_id=1, source_target_pairs={{0,4},{4,8},{8,12},{12,16},{16,20},{20,24},{24,28},{1,5},{5,9},{9,... | collective-permute-start | bytes 1769480 | tf_op jit(solution)/shard_map/ppermute | solution.py:20
  111.5 10.6 %collective-permute-start.10 = (f32[9,10,1,256]{3,1,2,0:T(8,128)S(1)}, f32[9,10,1,256]{3,1,2,0:T(8,128)S(1)}, u32[]{:S(2)}, u32[]{:S(2)}) collective-permute-start(f32[9,10,1,256]{3,1,2,0:T(8,128)S(1)} %copy.74), channel_id=1, source_target_pairs={{1,0},{2,1},{3,2},{5,4},{6,5},{7,6},{9,8},{10,9},{11,10},{13,12},{... | collective-permute-start | bytes 276488 | tf_op jit(solution)/shard_map/ppermute | solution.py:23
  113.4 8.7 %collective-permute-start.11 = (f32[9,10,1,256]{3,1,2,0:T(8,128)S(1)}, f32[9,10,1,256]{3,1,2,0:T(8,128)S(1)}, u32[]{:S(2)}, u32[]{:S(2)}) collective-permute-start(f32[9,10,1,256]{3,1,2,0:T(8,128)S(1)} %copy.76), channel_id=1, source_target_pairs={{0,1},{1,2},{2,3},{4,5},{5,6},{6,7},{8,9},{9,10},{10,11},{12,13},{... | collective-permute-start | bytes 276488 | tf_op jit(solution)/shard_map/ppermute | solution.py:20
  116.7 33.2 %all-to-all-start.1 = ((f32[8,16,256]{2,1,0:T(8,128)}), f32[8,16,256]{2,1,0:T(8,128)}, u32[]{:S(2)}, u32[]{:S(2)}) async-start(f32[8,16,256]{2,1,0:T(8,128)} %fusion.40), calls=%async_computation.1 | async-start | bytes 262144 | tf_op jit(solution)/shard_map/all_to_all | solution.py:115
  122.3 10.3 %copy-start.1 = (f32[8,8,64,256]{3,2,1,0:T(8,128)S(1)}, f32[8,8,64,256]{3,2,1,0:T(8,128)}, u32[]{:S(2)}) copy-start(f32[8,8,64,256]{3,2,1,0:T(8,128)} %copy-done) | copy-start | bytes 12582916
  144.1 7.6 %collective-permute-start.12 = (f32[1,64,256]{2,1,0:T(8,128)S(1)}, f32[1,64,256]{2,1,0:T(8,128)S(1)}, u32[]{:S(2)}, u32[]{:S(2)}) collective-permute-start(f32[1,64,256]{2,1,0:T(8,128)S(1)} %get-tuple-element.36), channel_id=1, source_target_pairs={{4,0},{8,4},{12,8},{16,12},{20,16},{24,20},{28,24},{5,1},{9,5},{13... | collective-permute-start | bytes 196616 | tf_op jit(solution)/shard_map/ppermute | solution.py:23
  147.5 7.1 %collective-permute-start.13 = (f32[1,64,256]{2,1,0:T(8,128)S(1)}, f32[1,64,256]{2,1,0:T(8,128)S(1)}, u32[]{:S(2)}, u32[]{:S(2)}) collective-permute-start(f32[1,64,256]{2,1,0:T(8,128)S(1)} %get-tuple-element.35), channel_id=1, source_target_pairs={{0,4},{4,8},{8,12},{12,16},{16,20},{20,24},{24,28},{1,5},{5,9},{9,... | collective-permute-start | bytes 196616 | tf_op jit(solution)/shard_map/ppermute | solution.py:20
  154.6 10.4 %collective-permute-start.14 = (f32[10,1,256]{2,1,0:T(1,128)S(1)}, f32[10,1,256]{2,1,0:T(1,128)S(1)}, u32[]{:S(2)}, u32[]{:S(2)}) collective-permute-start(f32[10,1,256]{2,1,0:T(1,128)S(1)} %get-tuple-element.32), channel_id=1, source_target_pairs={{1,0},{2,1},{3,2},{5,4},{6,5},{7,6},{9,8},{10,9},{11,10},{13,12},{... | collective-permute-start | bytes 30728 | tf_op jit(solution)/shard_map/ppermute | solution.py:23
  156.5 8.5 %collective-permute-start.15 = (f32[10,1,256]{2,1,0:T(1,128)S(1)}, f32[10,1,256]{2,1,0:T(1,128)S(1)}, u32[]{:S(2)}, u32[]{:S(2)}) collective-permute-start(f32[10,1,256]{2,1,0:T(1,128)S(1)} %get-tuple-element.31), channel_id=1, source_target_pairs={{0,1},{1,2},{2,3},{4,5},{5,6},{6,7},{8,9},{9,10},{10,11},{12,13},{... | collective-permute-start | bytes 30728 | tf_op jit(solution)/shard_map/ppermute | solution.py:20
  158.9 6.5 %copy-start.2 = (f32[8,64,256]{2,1,0:T(8,128)S(1)}, f32[8,64,256]{2,1,0:T(8,128)}, u32[]{:S(2)}) copy-start(f32[8,64,256]{2,1,0:T(8,128)} %get-tuple-element.6) | copy-start | bytes 1572868
where the time goes:
time: 172 us; the launch traced here: 170 us
  other arithmetic  70.5 us (41%)
  starting transfers between devices  52.4 us (30%)
  waiting for transfers between devices  36.9 us (21%)
  local copies, waits for them, and re-layouts  5.16 us (3%)
  matrix products  3.61 us (2%)
    ppermute x8, waiting for transfers between devices, extended_2(): lax.ppermute(lax.slice_in_dim(block, 0, width, axis=dim), axis, backward)  23.5 us
    ppermute x8, starting transfers between devices, extended_2(): lax.ppermute(lax.slice_in_dim(block, block.shape[dim] - width, None, axis...  22.1 us
    ppermute x8, starting transfers between devices, extended_2(): lax.ppermute(lax.slice_in_dim(block, 0, width, axis=dim), axis, backward)  19.5 us
    sub x2, other arithmetic, laplace(): return total - 6.0 * shifted(0, 0, 0)  16.6 us
    concatenate x7, other arithmetic, extended_2(): block = jnp.concatenate([low, block, high], axis=dim)  16.2 us
    ppermute x8, waiting for transfers between devices, extended_2(): lax.ppermute(lax.slice_in_dim(block, block.shape[dim] - width, None, axis...  13.4 us
    reduce_sum x1, other arithmetic, pointwise(): coupled = jnp.sum(lam_e * (phases * phases - phases), axis=0)  9.28 us
    add x1, other arithmetic, pointwise(): new_phases + 12.0 * barrier * lam_mu * (phases * phases - phases)  6.05 us
  transfers between devices with their start and end apart: 18, of which 7 were waited for; matrix products, arithmetic and copies ran while one was open for 40% of the time, Pallas kernels for 0%

commit v1 on v0

v1 whole, which is shorter than its diff:
```python
import functools

import jax
import jax.numpy as jnp
from jax import lax
from jax.experimental import pallas as pl
from jax.experimental.pallas import tpu as pltpu
from jax.sharding import PartitionSpec as P

TILE = 8
GRAIN_DEV = 8
DT = 0.05
MESH = pl.DeviceIdType.MESH
LM = 9


def kernel(
    n_gx, n_gy, cot, f1, f0, slot_grain, out, grad,
    cp, c1p, lmp, f1v, f0v, ov, s1, w1, k1, s0, w2, k2, yh, ys, part, gsend, grecv,
    send_sem, recv_sem, load_sem, store_sem, gsend_sem, grecv_sem,
):
    fields, cx, cy, nz = cot.shape
    slots = fields - 1
    gx, gy = lax.axis_index("gx"), lax.axis_index("gy")
    can_send = (gx < n_gx - 1, gx > 0, gy < n_gy - 1, gy > 0)
    can_recv = (gx > 0, gx < n_gx - 1, gy > 0, gy < n_gy - 1)
    target = (
        (jnp.minimum(gx + 1, n_gx - 1), gy),
        (jnp.maximum(gx - 1, 0), gy),
        (gx, jnp.minimum(gy + 1, n_gy - 1)),
        (gx, jnp.maximum(gy - 1, 0)),
    )

    def load(source, dest, index):
        return pltpu.make_async_copy(source, dest, load_sem.at[index])

    loads = [load(cot.at[k], cp.at[k, pl.ds(1, cx)], k) for k in range(fields)]
    load_f1, load_f0 = load(f1, f1v, fields), load(f0, f0v, fields + 1)
    for copy in loads:
        copy.start()
    load_f1.start()
    load_f0.start()

    def remote(step, k, side):
        if side < 2:
            padded = lmp.at[step] if k == LM else (c1p.at[k] if step else cp.at[k])
            dst = padded.at[0 if side == 0 else cx + 1]
            edge = cx - 1 if side == 0 else 0
            if step == 0 and k != LM:
                src = cot.at[k, edge]
            else:
                src = padded.at[edge + 1]
        else:
            src, dst = ys.at[step, k, side - 2], yh.at[step, k, side - 2]
        return pltpu.make_async_remote_copy(
            src_ref=src, dst_ref=dst, send_sem=send_sem.at[step, k, side],
            recv_sem=recv_sem.at[step, k, side], device_id=target[side], device_id_type=MESH,
        )

    def send(step, k, sides=(0, 1, 2, 3)):
        for side in sides:
            pl.when(can_send[side])(lambda side=side: remote(step, k, side).start())

    def sent(step, k):
        for side in range(4):
            pl.when(can_send[side])(lambda side=side: remote(step, k, side).wait_send())

    def recv(step, k):
        for side in range(4):
            pl.when(can_recv[side])(lambda side=side: remote(step, k, side).wait_recv())

    def clear_x(row):
        zero = jnp.zeros((cy, nz), jnp.float32)

        def body(k, _):
            cp[k, row] = zero
            c1p[k, row] = zero
            return 0

        lax.fori_loop(0, fields, body, 0)
        lmp[0, row] = zero
        lmp[1, row] = zero

    def clear_y(side):
        zero = jnp.zeros((cx, nz), jnp.float32)

        def body(k, _):
            yh[0, k, side] = zero
            yh[1, k, side] = zero
            return 0

        lax.fori_loop(0, fields + 1, body, 0)

    pl.when(gx == 0)(lambda: clear_x(0))
    pl.when(gx == n_gx - 1)(lambda: clear_x(cx + 1))
    pl.when(gy == 0)(lambda: clear_y(0))
    pl.when(gy == n_gy - 1)(lambda: clear_y(1))

    barrier = pltpu.get_barrier_semaphore()
    for d in range(1, n_gx):
        pl.semaphore_signal(barrier, inc=1, device_id=(lax.rem(gx + d, n_gx), gy), device_id_type=MESH)
    for side in (2, 3):
        def greet(side=side):
            pl.semaphore_signal(barrier, inc=1, device_id=target[side], device_id_type=MESH)
        pl.when(can_send[side])(greet)
    beside = (gy > 0).astype(jnp.int32) + (gy < n_gy - 1).astype(jnp.int32)
    pl.semaphore_wait(barrier, n_gx - 1 + beside)

    for k in range(3):
        send(0, k, (0, 1))

    row_id = lax.broadcasted_iota(jnp.int32, (cy, nz), 0)
    lane_id = lax.broadcasted_iota(jnp.int32, (cy, nz), 1)

    def lap(ref, low, high, x):
        v = ref[x + 1]
        total = ref[x] + ref[x + 2]
        total += jnp.where(row_id == 0, low[pl.ds(x, 1), :], pltpu.roll(v, 1, 0))
        total += jnp.where(row_id == cy - 1, high[pl.ds(x, 1), :], pltpu.roll(v, cy - 1, 0))
        total += jnp.where(lane_id == 0, 0.0, pltpu.roll(v, 1, 1))
        total += jnp.where(lane_id == nz - 1, 0.0, pltpu.roll(v, nz - 1, 1))
        return v, total - 6.0 * v

    def stage(step, k, x, v):
        ys[step, k, 0, pl.ds(x, 1), :] = v[cy - 1 : cy]
        ys[step, k, 1, pl.ds(x, 1), :] = v[0:1]

    def over_x(body, init=0):
        return lax.fori_loop(0, cx, body, init)

    def stage_cot(k):
        loads[k].wait()

        def body(x, _):
            stage(0, k, x, cp[k, x + 1])
            return 0

        over_x(body)
        send(0, k, (2, 3))

    for k in range(fields):
        stage_cot(k)

    def potential(step):
        ref = c1p if step else cp

        def body(x, _):
            _, value = lap(ref.at[0], yh.at[step, 0, 0], yh.at[step, 0, 1], x)
            value = DT * value
            lmp[step, x + 1] = value
            stage(step, LM, x, value)
            return 0

        over_x(body)

    def density(step):
        ref, field, coupled = (c1p, f0v, k2) if step else (cp, f1v, k1)

        def body(x, _):
            lam_mu, lap_mu = lap(lmp.at[step], yh.at[step, LM, 0], yh.at[step, LM, 1], x)
            c = field[0, x]
            curvature = 16.0 * (2.0 - 12.0 * c + 12.0 * c * c) + 2.0
            value = ref[0, x + 1] + lam_mu * curvature - lap_mu - (12.0 * DT) * coupled[x]
            if step:
                ov[0, x] = value
            else:
                c1p[0, x + 1] = value
                stage(1, 0, x, value)
            return 0

        over_x(body)

    def phase(step, s):
        ref, field, base, weighted = (c1p, f0v, s0, w2) if step else (cp, f1v, s1, w1)

        def body(x, total):
            v, lap_v = lap(ref.at[s], yh.at[step, s, 0], yh.at[step, s, 1], x)
            eta, c = field[s, x], field[0, x]
            inner = v * (base[x] - 2.0 * (2.0 - c) * eta) + 2.0 * eta * weighted[x]
            value = v - (12.0 * DT) * inner + DT * lap_v
            value += 12.0 * lmp[step, x + 1] * (eta * eta - eta)
            if step:
                ov[s, x] = value
                return total
            c1p[s, x + 1] = value
            stage(1, s, x, value)
            old = f0v[s, x]
            first, second = value * old, value * (old * old - old)
            w2[x] = first if s == 1 else w2[x] + first
            k2[x] = second if s == 1 else k2[x] + second
            return total + (v + value)

        if step:
            over_x(body)
        else:
            total = over_x(body, jnp.zeros((cy, nz), jnp.float32))
            rows = jnp.sum(total.reshape(cy // TILE, TILE, nz), axis=1)
            part[pl.ds((s - 1) * (cy // TILE), cy // TILE), :] = DT * rows

    def store(k):
        return pltpu.make_async_copy(ov.at[k], out.at[k], store_sem.at[k])

    load_f1.wait()
    load_f0.wait()

    def sums(x, _):
        zero = jnp.zeros((cy, nz), jnp.float32)

        def body(s, carry):
            square, square_old, weighted, coupled = carry
            eta, old, lam = f1v[s, x], f0v[s, x], cp[s, x + 1]
            product = lam * eta
            eta_square = eta * eta
            return (square + eta_square, square_old + old * old, weighted + product, coupled + lam * (eta_square - eta))

        square, square_old, weighted, coupled = lax.fori_loop(1, fields, body, (zero, zero, zero, zero))
        s1[x] = (1.0 - f1v[0, x]) + square
        s0[x] = (1.0 - f0v[0, x]) + square_old
        w1[x] = weighted
        k1[x] = coupled
        return 0

    def grain_exchange(d):
        peer = lax.rem(gx + d, n_gx)
        return pltpu.make_async_remote_copy(
            src_ref=gsend.at[peer], dst_ref=grecv.at[d],
            send_sem=gsend_sem.at[d], recv_sem=grecv_sem.at[d],
            device_id=(peer, gy), device_id_type=MESH,
        )

    def grains():
        grain = slot_grain[...]
        owner = lax.div(lax.div(grain, GRAIN_DEV), n_gy)
        key = owner * GRAIN_DEV + lax.rem(grain, GRAIN_DEV)
        tiles = key.shape[0]
        column = lax.broadcasted_iota(jnp.int32, (tiles, n_gx * GRAIN_DEV), 1)
        chosen = jnp.concatenate(
            [(column == key[:, s : s + 1]).astype(jnp.float32) for s in range(slots)], axis=0
        )
        summed = lax.dot_general(
            chosen, part[...], (((0,), (0,)), ((), ())),
            precision=lax.Precision.HIGHEST, preferred_element_type=jnp.float32,
        )
        gsend[...] = summed.reshape(n_gx, GRAIN_DEV, nz)
        for d in range(1, n_gx):
            grain_exchange(d).start()

    recv(0, 0)
    potential(0)
    send(0, LM)
    send(0, 3, (0, 1))
    over_x(sums)

    def first(s):
        recv(0, s)
        phase(0, s)

    first(1)
    send(0, 4, (0, 1))
    first(2)
    recv(0, LM)
    density(0)
    send(1, 0)
    send(0, 5, (0, 1))
    first(3)
    send(0, 6, (0, 1))
    first(4)
    recv(1, 0)
    potential(1)
    send(1, LM)
    send(0, 7, (0, 1))
    first(5)
    send(0, 8, (0, 1))
    first(6)
    send(1, 1)
    recv(1, LM)
    send(1, 2)
    first(7)
    send(1, 3)
    first(8)
    send(1, 4)
    grains()
    density(1)
    store(0).start()
    for s in range(1, fields):
        recv(1, s)
        if s + 4 < fields:
            send(1, s + 4)
        phase(1, s)
        store(s).start()

    total = gsend[gx]
    for d in range(1, n_gx):
        grain_exchange(d).wait_recv()
        total += grecv[d]
    grad[...] = total
    for d in range(1, n_gx):
        grain_exchange(d).wait_send()
    for step in range(2):
        for k in range(fields + 1):
            sent(step, k)
    for k in range(fields):
        store(k).wait()


def solution(mesh):
    n_gx, n_gy = mesh.shape["gx"], mesh.shape["gy"]

    def shards(cotangent, fields_one, fields_zero, slot_grain):
        fields, cx, cy, nz = cotangent.shape
        whole = pltpu.VMEM((fields, cx, cy, nz), jnp.float32)
        padded = pltpu.VMEM((fields, cx + 2, cy, nz), jnp.float32)
        single = pltpu.VMEM((cx, cy, nz), jnp.float32)
        rows = pltpu.VMEM((2, fields + 1, 2, cx, nz), jnp.float32)
        tiles = cx // TILE * (cy // TILE)
        row_count = tiles * slot_grain.shape[-1]
        anywhere = pl.BlockSpec(memory_space=pl.ANY)
        vmem = pl.BlockSpec(memory_space=pltpu.VMEM)
        return pl.pallas_call(
            functools.partial(kernel, n_gx, n_gy),
            out_shape=(
                jax.ShapeDtypeStruct(cotangent.shape, jnp.float32),
                jax.ShapeDtypeStruct((GRAIN_DEV, nz), jnp.float32),
            ),
            in_specs=[anywhere, anywhere, anywhere, vmem],
            out_specs=(anywhere, vmem),
            scratch_shapes=[
                padded, padded, pltpu.VMEM((2, cx + 2, cy, nz), jnp.float32),
                whole, whole, whole,
                single, single, single, single, single, single,
                rows, rows,
                pltpu.VMEM((row_count, nz), jnp.float32),
                pltpu.VMEM((n_gx, GRAIN_DEV, nz), jnp.float32),
                pltpu.VMEM((n_gx, GRAIN_DEV, nz), jnp.float32),
                pltpu.SemaphoreType.DMA((2, fields + 1, 4)),
                pltpu.SemaphoreType.DMA((2, fields + 1, 4)),
                pltpu.SemaphoreType.DMA((fields + 2,)),
                pltpu.SemaphoreType.DMA((fields,)),
                pltpu.SemaphoreType.DMA((n_gx,)),
                pltpu.SemaphoreType.DMA((n_gx,)),
            ],
            compiler_params=pltpu.CompilerParams(
                collective_id=0, has_side_effects=True, vmem_limit_bytes=56 * 1024 * 1024
            ),
            cost_estimate=pl.CostEstimate(
                flops=100 * cotangent.size, bytes_accessed=16 * cotangent.size, transcendentals=0
            ),
        )(cotangent, fields_one, fields_zero, slot_grain.reshape(tiles, -1))

    placed = (
        P(None, "gx", "gy", None),
        P(None, "gx", "gy", None),
        P(None, "gx", "gy", None),
        P("gx", "gy", None),
    )
    return jax.shard_map(
        shards,
        mesh=mesh,
        in_specs=placed,
        out_specs=(P(None, "gx", "gy", None), P(("gx", "gy"), None)),
        check_vma=False,
    )
```

time: 172 us -> 75.1 us (0.44); the launches traced: 170 us -> 74.9 us
  other arithmetic: 70.5 us -> 0 us
  Pallas kernels: 0 us -> 68.5 us
  starting transfers between devices: 52.4 us -> 0 us
  waiting for transfers between devices: 36.9 us -> 0 us
  matrix products: 3.61 us -> 0 us
    pallas_call x0 -> x1, Pallas kernels: none -> 68.5 us  [shards(): pl.pallas_call(functools.partial(kernel, n_gx, n_gy), out_shape=(jax.Shap...]
    ppermute x16 -> x0, starting transfers between devices: 41.6 us -> none  [the longest x8 22.1 us: extended_2(): lax.ppermute(lax.slice_in_dim(block, block.shape[dim] - width, None, axis...]
    ppermute x16 -> x0, waiting for transfers between devices: 36.9 us -> none  [the longest x8 23.5 us: extended_2(): lax.ppermute(lax.slice_in_dim(block, 0, width, axis=dim), axis, backward)]
    sub x5 -> x0, other arithmetic: 23.5 us -> none  [the longest x2 16.6 us: laplace(): return total - 6.0 * shifted(0, 0, 0)]
    concatenate x9 -> x0, other arithmetic: 18.8 us -> none  [the longest x7 16.2 us: extended_2(): block = jnp.concatenate([low, block, high], axis=dim)]
    reduce_sum x5 -> x0, other arithmetic: 14.9 us -> none  [the longest x1 9.28 us: pointwise(): coupled = jnp.sum(lam_e * (phases * phases - phases), axis=0)]
    all_to_all x2 -> x0, starting transfers between devices: 10.9 us -> none  [the longest x1 5.54 us: shards(): lax.all_to_all(labels, 'gx', split_axis=0, concat_axis=0, tiled=True)]
    add x3 -> x0, other arithmetic: 6.08 us -> none  [the longest x1 6.05 us: pointwise(): new_phases + 12.0 * barrier * lam_mu * (phases * phases - phases)]
  transfers between devices with their start and end apart: 18 -> 0, of which waited for: 7 -> 0; matrix products, arithmetic and copies ran while one was open for 40% -> 0% of each run, Pallas kernels for 0% -> 0%
where the time goes in v1:
time: 75.1 us; the launch traced here: 74.9 us
  Pallas kernels  68.5 us (91%)
  local copies, waits for them, and re-layouts  5.71 us (8%)
    pallas_call x1, Pallas kernels, shards(): pl.pallas_call(functools.partial(kernel, n_gx, n_gy), out_shape=(jax.Shap...  68.5 us
    unnamed x4, local copies, waits for them, and re-layouts  5.71 us

profile of v1, /device:TPU:10, one launch (start us, length us, event | category | flops | bytes accessed | tf_op | source)
XLA Modules:
  0.0 74.9 jit_solution(1929203252289187421)
XLA Ops:
  0.6 68.5 %shard_map.59 = (f32[9,8,64,256]{3,2,1,0:T(8,128)}, f32[8,256]{1,0:T(8,128)}) custom-call(f32[9,8,64,256]{3,2,1,0:T(8,128)} %cot.1, f32[9,8,64,256]{3,2,1,0:T(8,128)} %f1.1, f32[9,8,64,256]{3,2,1,0:T(8,128)} %f0.1, s32[8,8]{1,0:T(8,128)} %bitcast.1), custom_call_target="tpu_custom_call" | custom-call | flops 117964800 | bytes 18874368 | tf_op jit(solution)/shard_map/pallas_call | solution.py:319
  69.2 0.0 copy-start
  69.2 5.1 %copy.8 = f32[9,8,64,256]{3,2,1,0:T(8,128)} copy(f32[9,8,64,256]{3,2,1,0:T(8,128)} %get-tuple-element.4) | data formatting | bytes 9437184
  74.3 0.0 copy-done
  74.3 0.6 copy.9
Async XLA Ops:
  69.2 5.1 %copy-start = (f32[8,256]{1,0:T(8,128)S(1)}, f32[8,256]{1,0:T(8,128)}, u32[]{:S(2)}) copy-start(f32[8,256]{1,0:T(8,128)} %get-tuple-element.5) | copy-start | bytes 24580

commit v2 on v1

--- a/solution.py
+++ b/solution.py
@@ -16,8 +16,8 @@
 
 def kernel(
     n_gx, n_gy, cot, f1, f0, slot_grain, out, grad,
-    cp, c1p, lmp, f1v, f0v, ov, s1, w1, k1, s0, w2, k2, yh, ys, part, gsend, grecv,
-    send_sem, recv_sem, load_sem, store_sem, gsend_sem, grecv_sem,
+    cp, c1p, lmp, f1v, f0v, s1, w1, k1, s0, w2, k2, yh, ys, part, gsend, grecv,
+    send_sem, recv_sem, load_sem, gsend_sem, grecv_sem,
 ):
     fields, cx, cy, nz = cot.shape
     slots = fields - 1
@@ -106,7 +106,7 @@
     beside = (gy > 0).astype(jnp.int32) + (gy < n_gy - 1).astype(jnp.int32)
     pl.semaphore_wait(barrier, n_gx - 1 + beside)
 
-    for k in range(3):
+    for k in range(5):
         send(0, k, (0, 1))
 
     row_id = lax.broadcasted_iota(jnp.int32, (cy, nz), 0)
@@ -162,7 +162,7 @@
             curvature = 16.0 * (2.0 - 12.0 * c + 12.0 * c * c) + 2.0
             value = ref[0, x + 1] + lam_mu * curvature - lap_mu - (12.0 * DT) * coupled[x]
             if step:
-                ov[0, x] = value
+                out[0, x] = value
             else:
                 c1p[0, x + 1] = value
                 stage(1, 0, x, value)
@@ -180,7 +180,7 @@
             value = v - (12.0 * DT) * inner + DT * lap_v
             value += 12.0 * lmp[step, x + 1] * (eta * eta - eta)
             if step:
-                ov[s, x] = value
+                out[s, x] = value
                 return total
             c1p[s, x + 1] = value
             stage(1, s, x, value)
@@ -196,9 +196,6 @@
             total = over_x(body, jnp.zeros((cy, nz), jnp.float32))
             rows = jnp.sum(total.reshape(cy // TILE, TILE, nz), axis=1)
             part[pl.ds((s - 1) * (cy // TILE), cy // TILE), :] = DT * rows
-
-    def store(k):
-        return pltpu.make_async_copy(ov.at[k], out.at[k], store_sem.at[k])
 
     load_f1.wait()
     load_f0.wait()
@@ -248,46 +245,44 @@
     recv(0, 0)
     potential(0)
     send(0, LM)
-    send(0, 3, (0, 1))
+    send(0, 5, (0, 1))
     over_x(sums)
 
     def first(s):
         recv(0, s)
         phase(0, s)
 
-    first(1)
-    send(0, 4, (0, 1))
-    first(2)
+    for s in (1, 2, 3):
+        first(s)
+        send(0, s + 5, (0, 1))
+    first(4)
+    send(1, 1)
     recv(0, LM)
     density(0)
     send(1, 0)
-    send(0, 5, (0, 1))
-    first(3)
-    send(0, 6, (0, 1))
-    first(4)
+    for s in (5, 6, 7, 8):
+        first(s)
+        send(1, s - 3)
     recv(1, 0)
     potential(1)
     send(1, LM)
-    send(0, 7, (0, 1))
-    first(5)
-    send(0, 8, (0, 1))
-    first(6)
-    send(1, 1)
+    send(1, 6)
+    grains()
+
+    def second(s):
+        recv(1, s)
+        phase(1, s)
+
+    second(1)
+    send(1, 7)
+    second(2)
+    send(1, 8)
+    second(3)
+    second(4)
     recv(1, LM)
-    send(1, 2)
-    first(7)
-    send(1, 3)
-    first(8)
-    send(1, 4)
-    grains()
     density(1)
-    store(0).start()
-    for s in range(1, fields):
-        recv(1, s)
-        if s + 4 < fields:
-            send(1, s + 4)
-        phase(1, s)
-        store(s).start()
+    for s in (5, 6, 7, 8):
+        second(s)
 
     total = gsend[gx]
     for d in range(1, n_gx):
@@ -299,8 +294,6 @@
     for step in range(2):
         for k in range(fields + 1):
             sent(step, k)
-    for k in range(fields):
-        store(k).wait()
 
 
 def solution(mesh):
@@ -314,19 +307,19 @@
         rows = pltpu.VMEM((2, fields + 1, 2, cx, nz), jnp.float32)
         tiles = cx // TILE * (cy // TILE)
         row_count = tiles * slot_grain.shape[-1]
-        anywhere = pl.BlockSpec(memory_space=pl.ANY)
+        far = pl.BlockSpec(memory_space=pltpu.HBM)
         vmem = pl.BlockSpec(memory_space=pltpu.VMEM)
         return pl.pallas_call(
             functools.partial(kernel, n_gx, n_gy),
             out_shape=(
-                jax.ShapeDtypeStruct(cotangent.shape, jnp.float32),
+                pltpu.VMEM(cotangent.shape, jnp.float32),
                 jax.ShapeDtypeStruct((GRAIN_DEV, nz), jnp.float32),
             ),
-            in_specs=[anywhere, anywhere, anywhere, vmem],
-            out_specs=(anywhere, vmem),
+            in_specs=[far, far, far, vmem],
+            out_specs=(vmem, vmem),
             scratch_shapes=[
                 padded, padded, pltpu.VMEM((2, cx + 2, cy, nz), jnp.float32),
-                whole, whole, whole,
+                whole, whole,
                 single, single, single, single, single, single,
                 rows, rows,
                 pltpu.VMEM((row_count, nz), jnp.float32),
@@ -335,12 +328,11 @@
                 pltpu.SemaphoreType.DMA((2, fields + 1, 4)),
                 pltpu.SemaphoreType.DMA((2, fields + 1, 4)),
                 pltpu.SemaphoreType.DMA((fields + 2,)),
-                pltpu.SemaphoreType.DMA((fields,)),
                 pltpu.SemaphoreType.DMA((n_gx,)),
                 pltpu.SemaphoreType.DMA((n_gx,)),
             ],
             compiler_params=pltpu.CompilerParams(
-                collective_id=0, has_side_effects=True, vmem_limit_bytes=56 * 1024 * 1024
+                collective_id=0, has_side_effects=True, vmem_limit_bytes=48 * 1024 * 1024
             ),
             cost_estimate=pl.CostEstimate(
                 flops=100 * cotangent.size, bytes_accessed=16 * cotangent.size, transcendentals=0

time: 75.1 us -> 72.4 us (0.964)
  local copies, waits for them, and re-layouts: 5.71 us -> 3.47 us
    unnamed x4, local copies, waits for them, and re-layouts: 5.71 us -> 3.47 us
where the time goes in v2:
time: 72.4 us; the launch traced here: 72.2 us
  Pallas kernels  68.1 us (94%)
  local copies, waits for them, and re-layouts  3.47 us (5%)
    pallas_call x1, Pallas kernels, shards(): pl.pallas_call(functools.partial(kernel, n_gx, n_gy), out_shape=(pltpu.VM...  68.1 us
    unnamed x4, local copies, waits for them, and re-layouts  3.47 us

profile of v2, /device:TPU:10, one launch (start us, length us, event | category | flops | bytes accessed | tf_op | source)
XLA Modules:
  0.0 72.2 jit_solution(17243455820798036270)
XLA Ops:
  0.6 0.0 copy-start
  0.6 0.7 copy-done
  1.3 68.1 %shard_map.59 = (f32[9,8,64,256]{3,2,1,0:T(8,128)S(1)}, f32[8,256]{1,0:T(8,128)S(1)}) custom-call(f32[9,8,64,256]{3,2,1,0:T(8,128)} %cot.1, f32[9,8,64,256]{3,2,1,0:T(8,128)} %f1.1, f32[9,8,64,256]{3,2,1,0:T(8,128)} %f0.1, s32[8,8]{1,0:T(8,128)S(1)} %bitcast.1), custom_call_target="tpu_custom_call" | custom-call | flops 117964800 | bytes 18874368 | tf_op jit(solution)/shard_map/pallas_call | solution.py:312
  69.4 2.2 %copy.8 = f32[9,8,64,256]{3,2,1,0:T(8,128)} copy(f32[9,8,64,256]{3,2,1,0:T(8,128)S(1)} %get-tuple-element.2) | data formatting | bytes 9437184
  71.6 0.6 copy.9
Async XLA Ops:
  0.6 0.7 copy-start

commit v3 on v2

--- a/solution.py
+++ b/solution.py
@@ -16,7 +16,7 @@
 
 def kernel(
     n_gx, n_gy, cot, f1, f0, slot_grain, out, grad,
-    cp, c1p, lmp, f1v, f0v, s1, w1, k1, s0, w2, k2, yh, ys, part, gsend, grecv,
+    cp, c1p, lmp, f1v, f0v, s1, w1, k1, s0, w2, k2, yh, ys, part, gv, gsend, grecv,
     send_sem, recv_sem, load_sem, gsend_sem, grecv_sem,
 ):
     fields, cx, cy, nz = cot.shape
@@ -31,15 +31,24 @@
         (gx, jnp.maximum(gy - 1, 0)),
     )
 
+    barrier = pltpu.get_barrier_semaphore()
+    for d in range(1, n_gx):
+        pl.semaphore_signal(barrier, inc=1, device_id=(lax.rem(gx + d, n_gx), gy), device_id_type=MESH)
+    for side in (2, 3):
+        def greet(side=side):
+            pl.semaphore_signal(barrier, inc=1, device_id=target[side], device_id_type=MESH)
+        pl.when(can_send[side])(greet)
     def load(source, dest, index):
         return pltpu.make_async_copy(source, dest, load_sem.at[index])
 
     loads = [load(cot.at[k], cp.at[k, pl.ds(1, cx)], k) for k in range(fields)]
     load_f1, load_f0 = load(f1, f1v, fields), load(f0, f0v, fields + 1)
+    load_grain = load(slot_grain, gv, fields + 2)
     for copy in loads:
         copy.start()
     load_f1.start()
     load_f0.start()
+    load_grain.start()
 
     def remote(step, k, side):
         if side < 2:
@@ -96,13 +105,6 @@
     pl.when(gy == 0)(lambda: clear_y(0))
     pl.when(gy == n_gy - 1)(lambda: clear_y(1))
 
-    barrier = pltpu.get_barrier_semaphore()
-    for d in range(1, n_gx):
-        pl.semaphore_signal(barrier, inc=1, device_id=(lax.rem(gx + d, n_gx), gy), device_id_type=MESH)
-    for side in (2, 3):
-        def greet(side=side):
-            pl.semaphore_signal(barrier, inc=1, device_id=target[side], device_id_type=MESH)
-        pl.when(can_send[side])(greet)
     beside = (gy > 0).astype(jnp.int32) + (gy < n_gy - 1).astype(jnp.int32)
     pl.semaphore_wait(barrier, n_gx - 1 + beside)
 
@@ -226,7 +228,8 @@
         )
 
     def grains():
-        grain = slot_grain[...]
+        load_grain.wait()
+        grain = gv[...]
         owner = lax.div(lax.div(grain, GRAIN_DEV), n_gy)
         key = owner * GRAIN_DEV + lax.rem(grain, GRAIN_DEV)
         tiles = key.shape[0]
@@ -281,9 +284,10 @@
     second(4)
     recv(1, LM)
     density(1)
-    for s in (5, 6, 7, 8):
-        second(s)
-
+    second(5)
+    for k in range(fields + 1):
+        sent(0, k)
+    second(6)
     total = gsend[gx]
     for d in range(1, n_gx):
         grain_exchange(d).wait_recv()
@@ -291,9 +295,12 @@
     grad[...] = total
     for d in range(1, n_gx):
         grain_exchange(d).wait_send()
-    for step in range(2):
-        for k in range(fields + 1):
-            sent(step, k)
+    second(7)
+    for k in (0, 1, 2, 3, 4, 5, 6, LM):
+        sent(1, k)
+    second(8)
+    sent(1, 7)
+    sent(1, 8)
 
 
 def solution(mesh):
@@ -315,7 +322,7 @@
                 pltpu.VMEM(cotangent.shape, jnp.float32),
                 jax.ShapeDtypeStruct((GRAIN_DEV, nz), jnp.float32),
             ),
-            in_specs=[far, far, far, vmem],
+            in_specs=[far, far, far, far],
             out_specs=(vmem, vmem),
             scratch_shapes=[
                 padded, padded, pltpu.VMEM((2, cx + 2, cy, nz), jnp.float32),
@@ -323,11 +330,12 @@
                 single, single, single, single, single, single,
                 rows, rows,
                 pltpu.VMEM((row_count, nz), jnp.float32),
+                pltpu.VMEM((tiles, slot_grain.shape[-1]), jnp.int32),
                 pltpu.VMEM((n_gx, GRAIN_DEV, nz), jnp.float32),
                 pltpu.VMEM((n_gx, GRAIN_DEV, nz), jnp.float32),
                 pltpu.SemaphoreType.DMA((2, fields + 1, 4)),
                 pltpu.SemaphoreType.DMA((2, fields + 1, 4)),
-                pltpu.SemaphoreType.DMA((fields + 2,)),
+                pltpu.SemaphoreType.DMA((fields + 3,)),
                 pltpu.SemaphoreType.DMA((n_gx,)),
                 pltpu.SemaphoreType.DMA((n_gx,)),
             ],

time: 72.4 us -> 72.1 us (level)
  no operation moved by 1% of the time
where the time goes in v3:
time: 72.1 us; the launch traced here: 71.9 us
  Pallas kernels  67.8 us (94%)
  local copies, waits for them, and re-layouts  3.47 us (5%)
    pallas_call x1, Pallas kernels, shards(): pl.pallas_call(functools.partial(kernel, n_gx, n_gy), out_shape=(pltpu.VM...  67.8 us
    unnamed x4, local copies, waits for them, and re-layouts  3.47 us

profile of v3, /device:TPU:10, one launch (start us, length us, event | category | flops | bytes accessed | tf_op | source)
XLA Modules:
  0.0 71.9 jit_solution(6099823045054033446)
XLA Ops:
  0.6 0.0 copy-start
  0.6 0.7 copy-done
  1.3 67.8 %shard_map.59 = (f32[9,8,64,256]{3,2,1,0:T(8,128)S(1)}, f32[8,256]{1,0:T(8,128)S(1)}) custom-call(f32[9,8,64,256]{3,2,1,0:T(8,128)} %cot.1, f32[9,8,64,256]{3,2,1,0:T(8,128)} %f1.1, f32[9,8,64,256]{3,2,1,0:T(8,128)} %f0.1, s32[8,8]{1,0:T(8,128)S(1)} %bitcast.1), custom_call_target="tpu_custom_call" | custom-call | flops 117964800 | bytes 18874368 | tf_op jit(solution)/shard_map/pallas_call | solution.py:319
  69.1 2.2 %copy.8 = f32[9,8,64,256]{3,2,1,0:T(8,128)} copy(f32[9,8,64,256]{3,2,1,0:T(8,128)S(1)} %get-tuple-element.2) | data formatting | bytes 9437184
  71.3 0.6 copy.9
Async XLA Ops:
  0.6 0.7 copy-start

commit v4 on v3

--- a/solution.py
+++ b/solution.py
@@ -265,11 +265,16 @@
     send(1, 0)
     for s in (5, 6, 7, 8):
         first(s)
-        send(1, s - 3)
+        if s < 7:
+            send(1, 2 * s - 8)
+            send(1, 2 * s - 7)
+        elif s == 7:
+            send(1, 6)
     recv(1, 0)
     potential(1)
     send(1, LM)
-    send(1, 6)
+    send(1, 7)
+    send(1, 8)
     grains()
 
     def second(s):
@@ -277,9 +282,7 @@
         phase(1, s)
 
     second(1)
-    send(1, 7)
     second(2)
-    send(1, 8)
     second(3)
     second(4)
     recv(1, LM)

time: 72.1 us -> 74.3 us (1.031)
  Pallas kernels: 67.8 us -> 70 us
    pallas_call x1, Pallas kernels: 67.8 us -> 70 us  [shards(): pl.pallas_call(functools.partial(kernel, n_gx, n_gy), out_shape=(pltpu.VM...]
where the time goes in v4:
time: 74.3 us; the launch traced here: 74.2 us
  Pallas kernels  70 us (94%)
  local copies, waits for them, and re-layouts  3.47 us (5%)
    pallas_call x1, Pallas kernels, shards(): pl.pallas_call(functools.partial(kernel, n_gx, n_gy), out_shape=(pltpu.VM...  70 us
    unnamed x4, local copies, waits for them, and re-layouts  3.47 us

profile of v4, /device:TPU:10, one launch (start us, length us, event | category | flops | bytes accessed | tf_op | source)
XLA Modules:
  0.0 74.2 jit_solution(1191226935833970464)
XLA Ops:
  0.6 0.0 copy-start
  0.6 0.7 copy-done
  1.3 70.0 %shard_map.59 = (f32[9,8,64,256]{3,2,1,0:T(8,128)S(1)}, f32[8,256]{1,0:T(8,128)S(1)}) custom-call(f32[9,8,64,256]{3,2,1,0:T(8,128)} %cot.1, f32[9,8,64,256]{3,2,1,0:T(8,128)} %f1.1, f32[9,8,64,256]{3,2,1,0:T(8,128)} %f0.1, s32[8,8]{1,0:T(8,128)S(1)} %bitcast.1), custom_call_target="tpu_custom_call" | custom-call | flops 117964800 | bytes 18874368 | tf_op jit(solution)/shard_map/pallas_call | solution.py:322
  71.4 2.2 %copy.8 = f32[9,8,64,256]{3,2,1,0:T(8,128)} copy(f32[9,8,64,256]{3,2,1,0:T(8,128)S(1)} %get-tuple-element.2) | data formatting | bytes 9437184
  73.6 0.6 copy.9
Async XLA Ops:
  0.6 0.7 copy-start

commit v5 on v3

--- a/solution.py
+++ b/solution.py
@@ -108,7 +108,7 @@
     beside = (gy > 0).astype(jnp.int32) + (gy < n_gy - 1).astype(jnp.int32)
     pl.semaphore_wait(barrier, n_gx - 1 + beside)
 
-    for k in range(5):
+    for k in range(4):
         send(0, k, (0, 1))
 
     row_id = lax.broadcasted_iota(jnp.int32, (cy, nz), 0)
@@ -248,28 +248,26 @@
     recv(0, 0)
     potential(0)
     send(0, LM)
-    send(0, 5, (0, 1))
+    send(0, 4, (0, 1))
     over_x(sums)
 
     def first(s):
         recv(0, s)
         phase(0, s)
 
-    for s in (1, 2, 3):
+    for s in (1, 2, 3, 4):
         first(s)
-        send(0, s + 5, (0, 1))
-    first(4)
-    send(1, 1)
+        send(0, s + 4, (0, 1))
     recv(0, LM)
     density(0)
     send(1, 0)
     for s in (5, 6, 7, 8):
         first(s)
-        send(1, s - 3)
+        send(1, s - 4)
     recv(1, 0)
     potential(1)
     send(1, LM)
-    send(1, 6)
+    send(1, 5)
     grains()
 
     def second(s):
@@ -277,10 +275,11 @@
         phase(1, s)
 
     second(1)
+    send(1, 6)
+    second(2)
     send(1, 7)
-    second(2)
+    second(3)
     send(1, 8)
-    second(3)
     second(4)
     recv(1, LM)
     density(1)

time: 72.1 us -> 71.5 us (level)
  no operation moved by 1% of the time
where the time goes in v5:
time: 71.5 us; the launch traced here: 71.3 us
  Pallas kernels  67.2 us (94%)
  local copies, waits for them, and re-layouts  3.47 us (5%)
    pallas_call x1, Pallas kernels, shards(): pl.pallas_call(functools.partial(kernel, n_gx, n_gy), out_shape=(pltpu.VM...  67.2 us
    unnamed x4, local copies, waits for them, and re-layouts  3.47 us

profile of v5, /device:TPU:10, one launch (start us, length us, event | category | flops | bytes accessed | tf_op | source)
XLA Modules:
  0.0 71.3 jit_solution(4317584042966043675)
XLA Ops:
  0.6 0.0 copy-start
  0.6 0.7 copy-done
  1.3 67.2 %shard_map.59 = (f32[9,8,64,256]{3,2,1,0:T(8,128)S(1)}, f32[8,256]{1,0:T(8,128)S(1)}) custom-call(f32[9,8,64,256]{3,2,1,0:T(8,128)} %cot.1, f32[9,8,64,256]{3,2,1,0:T(8,128)} %f1.1, f32[9,8,64,256]{3,2,1,0:T(8,128)} %f0.1, s32[8,8]{1,0:T(8,128)S(1)} %bitcast.1), custom_call_target="tpu_custom_call" | custom-call | flops 117964800 | bytes 18874368 | tf_op jit(solution)/shard_map/pallas_call | solution.py:318
  68.5 2.2 %copy.8 = f32[9,8,64,256]{3,2,1,0:T(8,128)} copy(f32[9,8,64,256]{3,2,1,0:T(8,128)S(1)} %get-tuple-element.2) | data formatting | bytes 9437184
  70.7 0.6 copy.9
Async XLA Ops:
  0.6 0.7 copy-start
